TPU v7x, 32 devices: a whole 2x2x4 slice. The times are simulated.
32 devices in a mesh: row: 8 (over z, x), col: 4 (over y, core).
Axes of the slice: x: 2, y: 2, z: 4, core: 2. Of those that a mesh axis runs over, the one named last changes fastest.
Arguments:
- object_field: float32 [4, 2, 1024, 512], P(None, None, 'row', 'col'), may hold values from -5 to 5
- probe_wave: float32 [2, 128, 128], replicated, may hold values from -6 to 6
- positions: int32 [8, 4, 2, 2], P('row', 'col'), may hold values from 0 to 1023, as said below
- counts: int32 [8, 4], P('row', 'col'), may hold values from 0 to 2, as said below
- measured: float32 [8, 4, 2, 128, 128], P('row', 'col'), may hold values from 0 to 2
Outputs:
- object_grad: float32 [4, 2, 1024, 512], P(None, None, 'row', 'col')
- probe_grad: float32 [2, 128, 128], replicated
Inputs may be any that keep to these rules, and one draw needn't show every extreme that they name: positions[r, c, s] lies inside tile (r, c): its row in r * 128 to (r + 1) * 128 - 1 and its column in c * 128 to (c + 1) * 128 - 1; dead slots hold such positions too. `counts`: some tile has 2 live slots.
All inputs are finite; a program needn't handle non-finite values.
Results may differ from a plain program's by a relative error of at most 0.0003.
Values sent between devices are 32-bit elements; how exact they have to be, the bound alone decides.
A program may use at most 64 MiB of HBM per device.

v0:
```python
import math

import jax
import jax.numpy as jnp
from jax import lax
from jax.sharding import PartitionSpec as P

FRESNEL = 0.01


def with_halo(array, sides, width):
    for axis, dim in sides:
        peers, length = (lax.axis_size(axis), array.shape[dim])
        up = [(i, (i + 1) % peers) for i in range(peers - 1)]
        down = [(j, i) for i, j in up]
        last = lax.slice_in_dim(array, length - width, length, axis=dim)
        initial = lax.slice_in_dim(array, 0, width, axis=dim)
        before = lax.ppermute(last, axis, up)
        after = lax.ppermute(initial, axis, down)
        array = jnp.concatenate([before, array, after], axis=dim)
    return array


def matmul_exact(left, right):
    return jnp.dot(left, right, precision=lax.Precision.HIGHEST, preferred_element_type=jnp.float32)


def complex_matmul(left_real, left_imag, right_real, right_imag):
    real_out = matmul_exact(left_real, right_real) - matmul_exact(left_imag, right_imag)
    imag_out = matmul_exact(left_real, right_imag) + matmul_exact(left_imag, right_real)
    return (real_out, imag_out)


def transform(real_part, imag_part, table_real, table_imag):
    first_real, first_imag = complex_matmul(table_real, table_imag, real_part, imag_part)
    return complex_matmul(first_real, first_imag, table_real, table_imag)


def make_tables(points):
    indices = jnp.arange(points, dtype=jnp.int32)
    product = indices[:, None] * indices[None, :] % points
    phase_angle = 2.0 * math.pi / points * product.astype(jnp.float32)
    norm_scale = 1.0 / math.sqrt(points)
    table_real = jnp.cos(phase_angle) * norm_scale
    table_imag = -jnp.sin(phase_angle) * norm_scale
    frequency = jnp.where(indices < points // 2, indices, indices - points).astype(jnp.float32)
    prop_phase = -FRESNEL * (frequency[:, None] ** 2 + frequency[None, :] ** 2)
    return (table_real, table_imag, jnp.cos(prop_phase), jnp.sin(prop_phase))


def position_loss(patch_stack, probe_wave, measured_one, tables):
    table_real, table_imag, prop_real, prop_imag = tables
    wave_real = probe_wave[0]
    wave_imag = probe_wave[1]
    slice_count = patch_stack.shape[0]
    for depth_index in range(slice_count):
        trans_real = patch_stack[depth_index, 0]
        trans_imag = patch_stack[depth_index, 1]
        exit_real = wave_real * trans_real - wave_imag * trans_imag
        exit_imag = wave_real * trans_imag + wave_imag * trans_real
        far_real, far_imag = transform(exit_real, exit_imag, table_real, table_imag)
        if depth_index + 1 < slice_count:
            moved_real = far_real * prop_real - far_imag * prop_imag
            moved_imag = far_real * prop_imag + far_imag * prop_real
            wave_real, wave_imag = transform(moved_real, moved_imag, table_real, -table_imag)
    amplitude = jnp.sqrt(far_real * far_real + far_imag * far_imag + 1.0)
    return jnp.sum((amplitude - measured_one) ** 2)


def per_device(object_field, probe_wave, positions, counts, measured):
    slice_count = object_field.shape[0]
    probe_size = probe_wave.shape[-1]
    half_probe = probe_size // 2
    tile_rows = object_field.shape[2]
    tile_cols = object_field.shape[3]
    tables = make_tables(probe_size)
    padded = with_halo(object_field, (("row", 2), ("col", 3)), half_probe)
    corner = jnp.stack([lax.axis_index("row") * tile_rows, lax.axis_index("col") * tile_cols])
    local_starts = positions[0, 0] - corner[None, :]
    my_count = counts[0, 0]
    patterns = measured[0, 0]
    gradient = jax.grad(position_loss, argnums=(0, 1))
    anchor = jnp.zeros((), jnp.int32)

    def visit(slot_index, state_pair):
        object_sum, probe_sum = state_pair
        centre = lax.dynamic_index_in_dim(local_starts, slot_index, 0, keepdims=False)
        pattern = lax.dynamic_index_in_dim(patterns, slot_index, 0, keepdims=False)
        starts = (anchor, anchor, centre[0], centre[1])
        patch_stack = lax.dynamic_slice(padded, starts, (slice_count, 2, probe_size, probe_size))
        patch_grad, wave_grad = gradient(patch_stack, probe_wave, pattern, tables)
        weight = (slot_index < my_count).astype(jnp.float32)
        current = lax.dynamic_slice(object_sum, starts, (slice_count, 2, probe_size, probe_size))
        object_sum = lax.dynamic_update_slice(object_sum, current + weight * patch_grad, starts)
        return (object_sum, probe_sum + weight * wave_grad)

    initial = (jnp.zeros(padded.shape, jnp.float32), jnp.zeros(probe_wave.shape, jnp.float32))
    object_sum, probe_sum = lax.fori_loop(0, local_starts.shape[0], visit, initial)
    stacked = jnp.concatenate(
        [object_sum[:, :, :half_probe], object_sum[:, :, -half_probe:]], axis=2
    )
    arrived = with_halo(stacked, (("row", 2),), half_probe)
    middle = object_sum[:, :, half_probe : half_probe + tile_rows]
    middle = middle.at[:, :, :half_probe].add(arrived[:, :, :half_probe])
    middle = middle.at[:, :, tile_rows - half_probe :].add(arrived[:, :, 3 * half_probe :])
    beside = jnp.concatenate([middle[:, :, :, :half_probe], middle[:, :, :, -half_probe:]], axis=3)
    received = with_halo(beside, (("col", 3),), half_probe)
    result = middle[:, :, :, half_probe : half_probe + tile_cols]
    result = result.at[:, :, :, :half_probe].add(received[:, :, :, :half_probe])
    result = result.at[:, :, :, tile_cols - half_probe :].add(received[:, :, :, 3 * half_probe :])
    probe_grad_all = lax.psum(probe_sum, ("row", "col"))
    return (result, probe_grad_all)


def solution(mesh):
    in_specs = (
        P(None, None, "row", "col"),
        P(),
        P("row", "col", None, None),
        P("row", "col"),
        P("row", "col", None, None, None),
    )
    out_specs = (P(None, None, "row", "col"), P())
    return jax.shard_map(
        per_device, mesh=mesh, in_specs=in_specs, out_specs=out_specs, check_vma=False
    )
```

profile of v0, /device:TPU:0, one launch (start us, length us, event | category | flops | bytes accessed | tf_op | source)
XLA Modules:
  0.0 373.0 jit_solution(12624398460381422630)
XLA Ops:
  7.2 1.2 copy.63
  8.7 4.9 %collective-permute-start = (f32[4,2,64,128]{2,3,1,0:T(8,128)S(1)}, f32[4,2,64,128]{2,3,1,0:T(8,128)S(1)}, u32[]{:S(2)}, u32[]{:S(2)}) collective-permute-start(f32[4,2,64,128]{2,3,1,0:T(8,128)S(1)} %get-tuple-element.1041), channel_id=1, source_target_pairs={{0,4},{4,8},{8,12},{12,16},{16,20},{20,24},{24,28},{1,5},{5,9},{9,... | collective-permute-start | bytes 786440 | tf_op jit(solution)/shard_map/ppermute | solution.py:18
  13.6 1.3 collective-permute-start.1
  14.8 21.1 %collective-permute-done = f32[4,2,64,128]{2,3,1,0:T(8,128)S(1)} collective-permute-done((f32[4,2,64,128]{2,3,1,0:T(8,128)S(1)}, f32[4,2,64,128]{2,3,1,0:T(8,128)S(1)}, u32[]{:S(2)}, u32[]{:S(2)}) %collective-permute-start) | collective-permute-done | bytes 262176 | tf_op jit(solution)/shard_map/ppermute | solution.py:18
  36.4 1.1 fusion.777
  37.5 1.3 collective-permute-start.2
  38.8 1.3 collective-permute-start.3
  40.5 4.0 %collective-permute-done.3 = f32[4,2,256,64]{2,3,1,0:T(8,128)S(1)} collective-permute-done((f32[4,2,256,64]{2,3,1,0:T(8,128)}, f32[4,2,256,64]{2,3,1,0:T(8,128)S(1)}, u32[]{:S(2)}, u32[]{:S(2)}) %collective-permute-start.3) | collective-permute-done | bytes 524320 | tf_op jit(solution)/shard_map/ppermute | solution.py:19
  44.5 1.8 pad_maximum_fusion
  47.3 161.5 %while.24 = (s32[]{:T(128)}, f32[4,2,256,256]{3,2,1,0:T(8,128)S(1)}, f32[2,128,128]{2,1,0:T(8,128)S(1)}, s32[2,2]{1,0:T(2,128)S(1)}, s32[]{:T(128)}, /*index=5*/...) while((s32[]{:T(128)}, ...), condition=%wide.region_1.2_spmd.clone.clone.clone.clone, body=%wide.region_0.1_spmd.clone.clone.clone.clone.sunk | while | flops 2853437440 | bytes 28979552 | solution.py:98
  52.2 1.5 constant_dynamic-slice_fusion.9
  59.3 0.8 convolution_add_fusion.71
  60.2 0.8 fusion.1200
  61.0 0.8 convolution_subtract_fusion.27
  68.4 1.3 convolution_add_fusion.75
  69.8 0.8 fusion.1209
  70.6 0.8 convolution_subtract_fusion.30
  78.0 0.8 convolution_add_fusion.79
  78.9 0.8 fusion.1218
  79.7 0.8 convolution_subtract_fusion.33
  114.6 1.2 convolution_add_fusion.95
  119.7 7.2 %dynamic_update_slice.13 = f32[4,2,256,256]{3,2,1,0:T(8,128)S(1)} dynamic-update-slice(f32[4,2,256,256]{3,2,1,0:T(8,128)S(1)} %get-tuple-element.1192, f32[4,2,128,128]{3,2,1,0:T(8,128)S(1)} %multiply_add_fusion.2, s32[]{:T(128)} %constant.200.clone.1..sunk, s32[]{:T(128)} %constant.200.clone.1..sunk, s32[]{:T(128)S(6)} %select_n.714, s32[]{:T(128)S(6)} %select_n.715) | dynamic-update-slice | bytes 1048580 | tf_op jit(solution)/shard_map/while/body/eval_jaxpr/dynamic_update_slice | solution.py:94
  132.0 1.5 constant_dynamic-slice_fusion.9
  138.3 0.8 fusion.1202
  139.1 0.8 convolution_add_fusion.71
  139.9 0.8 fusion.1200
  140.8 0.8 convolution_subtract_fusion.27
  148.2 1.0 convolution_add_fusion.75
  149.2 0.8 fusion.1209
  150.1 0.8 convolution_subtract_fusion.30
  156.7 0.8 fusion.1220
  157.5 0.8 convolution_add_fusion.79
  158.3 0.8 fusion.1218
  159.1 0.8 convolution_subtract_fusion.33
  163.4 0.9 convolution_add_fusion.81
  194.3 1.0 convolution_add_fusion.95
  199.2 6.7 %dynamic_update_slice.13 = f32[4,2,256,256]{3,2,1,0:T(8,128)S(1)} dynamic-update-slice(f32[4,2,256,256]{3,2,1,0:T(8,128)S(1)} %get-tuple-element.1192, f32[4,2,128,128]{3,2,1,0:T(8,128)S(1)} %multiply_add_fusion.2, s32[]{:T(128)} %constant.200.clone.1..sunk, s32[]{:T(128)} %constant.200.clone.1..sunk, s32[]{:T(128)S(6)} %select_n.714, s32[]{:T(128)S(6)} %select_n.715) | dynamic-update-slice | bytes 1048580 | tf_op jit(solution)/shard_map/while/body/eval_jaxpr/dynamic_update_slice | solution.py:94
  208.9 4.5 %collective-permute-start.4 = (f32[4,2,64,256]{3,2,1,0:T(8,128)S(1)}, f32[4,2,64,256]{3,2,1,0:T(8,128)S(1)}, u32[]{:S(2)}, u32[]{:S(2)}) collective-permute-start(f32[4,2,64,256]{3,2,1,0:T(8,128)S(1)} %get-tuple-element.1036), channel_id=1, source_target_pairs={{0,4},{4,8},{8,12},{12,16},{16,20},{20,24},{24,28},{1,5},{5,9},{9,... | collective-permute-start | bytes 1572872 | tf_op jit(solution)/shard_map/ppermute | solution.py:18
  213.4 1.3 collective-permute-start.5
  214.8 17.6 %collective-permute-done.4 = f32[4,2,64,256]{3,2,1,0:T(8,128)S(1)} collective-permute-done((f32[4,2,64,256]{3,2,1,0:T(8,128)S(1)}, f32[4,2,64,256]{3,2,1,0:T(8,128)S(1)}, u32[]{:S(2)}, u32[]{:S(2)}) %collective-permute-start.4) | collective-permute-done | bytes 524320 | tf_op jit(solution)/shard_map/ppermute | solution.py:18
  232.6 0.9 fusion.776
  233.6 6.6 %collective-permute-start.6 = (f32[4,2,128,64]{3,2,1,0:T(8,128)S(1)}, f32[4,2,128,64]{3,2,1,0:T(8,128)S(1)}, u32[]{:S(2)}, u32[]{:S(2)}) collective-permute-start(f32[4,2,128,64]{3,2,1,0:T(8,128)S(1)} %get-tuple-element.1038), channel_id=1, source_target_pairs={{0,1},{1,2},{2,3},{4,5},{5,6},{6,7},{8,9},{9,10},{10,11},{12,13},{... | collective-permute-start | bytes 786440 | tf_op jit(solution)/shard_map/ppermute | solution.py:18
  240.4 1.3 collective-permute-start.7
  241.9 1.0 scatter-add.16
  242.9 1.4 collective-permute-done.7
  244.6 2.6 scatter-add.19
  247.2 117.1 %all-reduce.12.cloned.1.call-done = f32[2,128,128]{2,1,0:T(8,128)} async-done(((f32[2,128,128]{2,1,0:T(8,128)}), f32[2,128,128]{2,1,0:T(8,128)}) %all-reduce.12.cloned.1.call-update) | async-done | bytes 131088 | tf_op jit(solution)/shard_map/psum | solution.py:111
  364.3 1.6 copy.135
  (257 shorter events, 114.4 us)
Async XLA Ops:
  7.2 357.1 %all-reduce.12.cloned.1.call-start = ((), (), s32[]{:S(2)}) async-start(), calls=%async_computation | async-start | bytes 262144 | tf_op jit(solution)/shard_map/psum | solution.py:111
  8.7 27.2 %collective-permute-start = (f32[4,2,64,128]{2,3,1,0:T(8,128)S(1)}, f32[4,2,64,128]{2,3,1,0:T(8,128)S(1)}, u32[]{:S(2)}, u32[]{:S(2)}) collective-permute-start(f32[4,2,64,128]{2,3,1,0:T(8,128)S(1)} %get-tuple-element.1041), channel_id=1, source_target_pairs={{0,4},{4,8},{8,12},{12,16},{16,20},{20,24},{24,28},{1,5},{5,9},{9,... | collective-permute-start | bytes 786440 | tf_op jit(solution)/shard_map/ppermute | solution.py:18
  13.5 26.7 %copy-start.3 = (s32[1,1,2,2]{3,2,1,0:T(2,128)S(1)}, s32[1,1,2,2]{3,2,1,0:T(2,128)}, u32[]{:S(2)}) copy-start(s32[1,1,2,2]{3,2,1,0:T(2,128)} %param.17) | copy-start | bytes 52
  13.6 22.4 %collective-permute-start.1 = (f32[4,2,64,128]{2,3,1,0:T(8,128)S(1)}, f32[4,2,64,128]{2,3,1,0:T(8,128)S(1)}, u32[]{:S(2)}, u32[]{:S(2)}) collective-permute-start(f32[4,2,64,128]{2,3,1,0:T(8,128)S(1)} %get-tuple-element.1042), channel_id=1, source_target_pairs={{4,0},{8,4},{12,8},{16,12},{20,16},{24,20},{28,24},{5,1},{9,5},{13... | collective-permute-start | bytes 786440 | tf_op jit(solution)/shard_map/ppermute | solution.py:19
  37.5 3.0 collective-permute-start.2
  38.8 5.7 %collective-permute-start.3 = (f32[4,2,256,64]{2,3,1,0:T(8,128)}, f32[4,2,256,64]{2,3,1,0:T(8,128)S(1)}, u32[]{:S(2)}, u32[]{:S(2)}) collective-permute-start(f32[4,2,256,64]{2,3,1,0:T(8,128)} %get-tuple-element.1040), channel_id=1, source_target_pairs={{1,0},{2,1},{3,2},{5,4},{6,5},{7,6},{9,8},{10,9},{11,10},{13,12},{... | collective-permute-start | bytes 1572872 | tf_op jit(solution)/shard_map/ppermute | solution.py:19
  46.4 0.9 copy-start
  46.4 1.0 copy-start.4
  208.8 6.0 %copy-start.1 = (f32[2,128,128]{2,1,0:T(8,128)}, f32[2,128,128]{2,1,0:T(8,128)S(1)}, u32[]{:S(2)}) copy-start(f32[2,128,128]{2,1,0:T(8,128)S(1)} %get-tuple-element.697) | copy-start | bytes 393220
  208.9 23.5 %collective-permute-start.4 = (f32[4,2,64,256]{3,2,1,0:T(8,128)S(1)}, f32[4,2,64,256]{3,2,1,0:T(8,128)S(1)}, u32[]{:S(2)}, u32[]{:S(2)}) collective-permute-start(f32[4,2,64,256]{3,2,1,0:T(8,128)S(1)} %get-tuple-element.1036), channel_id=1, source_target_pairs={{0,4},{4,8},{8,12},{12,16},{16,20},{20,24},{24,28},{1,5},{5,9},{9,... | collective-permute-start | bytes 1572872 | tf_op jit(solution)/shard_map/ppermute | solution.py:18
  213.4 19.1 %collective-permute-start.5 = (f32[4,2,64,256]{3,2,1,0:T(8,128)S(1)}, f32[4,2,64,256]{3,2,1,0:T(8,128)S(1)}, u32[]{:S(2)}, u32[]{:S(2)}) collective-permute-start(f32[4,2,64,256]{3,2,1,0:T(8,128)S(1)} %get-tuple-element.1035), channel_id=1, source_target_pairs={{4,0},{8,4},{12,8},{16,12},{20,16},{24,20},{28,24},{5,1},{9,5},{13... | collective-permute-start | bytes 1572872 | tf_op jit(solution)/shard_map/ppermute | solution.py:19
  233.6 8.1 %collective-permute-start.6 = (f32[4,2,128,64]{3,2,1,0:T(8,128)S(1)}, f32[4,2,128,64]{3,2,1,0:T(8,128)S(1)}, u32[]{:S(2)}, u32[]{:S(2)}) collective-permute-start(f32[4,2,128,64]{3,2,1,0:T(8,128)S(1)} %get-tuple-element.1038), channel_id=1, source_target_pairs={{0,1},{1,2},{2,3},{4,5},{5,6},{6,7},{8,9},{9,10},{10,11},{12,13},{... | collective-permute-start | bytes 786440 | tf_op jit(solution)/shard_map/ppermute | solution.py:18
  240.4 4.0 %collective-permute-start.7 = (f32[4,2,128,64]{3,2,1,0:T(8,128)}, f32[4,2,128,64]{3,2,1,0:T(8,128)S(1)}, u32[]{:S(2)}, u32[]{:S(2)}) collective-permute-start(f32[4,2,128,64]{3,2,1,0:T(8,128)} %get-tuple-element.1037), channel_id=1, source_target_pairs={{1,0},{2,1},{3,2},{5,4},{6,5},{7,6},{9,8},{10,9},{11,10},{13,12},{... | collective-permute-start | bytes 786440 | tf_op jit(solution)/shard_map/ppermute | solution.py:19
  247.2 118.7 %copy-start.2 = (f32[4,2,128,128]{3,2,1,0:T(8,128)}, f32[4,2,128,128]{3,2,1,0:T(8,128)S(1)}, u32[]{:S(2)}) copy-start(f32[4,2,128,128]{3,2,1,0:T(8,128)S(1)} %scatter-add.19) | copy-start | bytes 1572868
Sparse Core Ops, SparseCore 0:
  240.3 123.9 all-reduce.11
where the time goes:
time: 376 us; the launch traced here: 373 us
  waiting for transfers between devices  162 us (43%)
  matrix products  128 us (34%)
  local copies, waits for them, and re-layouts  29.7 us (8%)
  starting transfers between devices  22.4 us (6%)
  between operations  14.6 us (4%)
  loops' own time  13 us (3%)
    dot_general x224, matrix products, matmul_exact(): jnp.dot(left, right, precision=lax.Precision.HIGHEST, preferred_element_t...  128 us
    psum x1, waiting for transfers between devices, per_device(): probe_grad_all = lax.psum(probe_sum, ('row', 'col'))  117 us
    ppermute x4, waiting for transfers between devices, with_halo(): before = lax.ppermute(last, axis, up)  38.9 us
    ppermute x4, starting transfers between devices, with_halo(): before = lax.ppermute(last, axis, up)  17.2 us
    dynamic_update_slice x2, local copies, waits for them, and re-layouts, visit(): lax.dynamic_update_slice(object_sum, current + weight * patch_grad, starts)  13.9 us
    another operation x1, loops' own time, per_device(): lax.fori_loop(0, local_starts.shape[0], visit, initial)  13 us
  transfers between devices with their start and end apart: 9, of which 6 were waited for; matrix products, arithmetic and copies ran while one was open for 1% of the time, Pallas kernels for 0%

commit v1 on v0

v1 whole, which is shorter than its diff:
```python
import functools
import math

import jax
import jax.numpy as jnp
import numpy as np
from jax import lax
from jax.experimental import pallas as pl
from jax.experimental.pallas import tpu as pltpu
from jax.sharding import PartitionSpec as P

FRESNEL = 0.01
MESH = pl.DeviceIdType.MESH


def tables(points):
    index = np.arange(points)
    dft = np.exp(-2j * math.pi * ((index[:, None] * index[None, :]) % points) / points) / math.sqrt(points)
    freq = np.where(index < points // 2, index, index - points).astype(np.float64)
    step = np.conj(dft) @ (np.exp(-1j * FRESNEL * freq**2)[:, None] * dft)
    blocks = []
    for m in (step, dft):
        right = np.block([[m.real, m.imag], [-m.imag, m.real]])
        left = np.block([[m.real, -m.imag], [m.imag, m.real]])
        blocks += [right, left]
    full = np.stack(blocks).astype(np.float32)
    high = full.astype(jnp.bfloat16)
    low = (full - high.astype(np.float32)).astype(jnp.bfloat16)
    return np.stack([high, low], axis=1)


def split(x):
    high = x.astype(jnp.bfloat16)
    return high, (x - high.astype(jnp.float32)).astype(jnp.bfloat16)


def dot(a, b):
    return jnp.dot(a, b, preferred_element_type=jnp.float32)


def kernel(R, C, pos, cnt, obj, probe, meas, mats, out, pg_out,
           row_in, col_send, col_in, padded, patch, wave, zpad, g_send, g_in, m_send, m_in,
           pg, s1, q1, s2, q2, f2,
           hs_sem, hr_sem, as_sem, ar_sem, bs_sem, br_sem):
    K = obj.shape[0]
    N = obj.shape[-1]
    H = N // 2
    S = meas.shape[2]
    r = lax.axis_index("row")
    c = lax.axis_index("col")

    barrier = pltpu.get_barrier_semaphore()
    for j in range(1, R):
        pl.semaphore_signal(barrier, inc=1, device_id=(lax.rem(r + j, R), c), device_id_type=MESH)
    for j in range(1, C):
        pl.semaphore_signal(barrier, inc=1, device_id=(r, lax.rem(c + j, C)), device_id_type=MESH)
    pl.semaphore_wait(barrier, R + C - 2)

    have = {"up": r > 0, "down": r < R - 1, "left": c > 0, "right": c < C - 1}
    where_to = {"up": (r - 1, c), "down": (r + 1, c), "left": (r, c - 1), "right": (r, c + 1)}
    back = {"up": "down", "down": "up", "left": "right", "right": "left"}
    slot = {"up": 0, "down": 1, "left": 0, "right": 1}

    def row_refs(k, side):
        rows = pl.ds(0, H) if side == "up" else pl.ds(H, H)
        return obj.at[k, :, rows, :], row_in.at[k, slot[back[side]]]

    def own_refs(k, side):
        return col_send.at[k, slot[side], 0], col_in.at[k, slot[back[side]], 0]

    def halo_refs(k, side):
        return col_send.at[k, slot[side], 1], col_in.at[k, slot[back[side]], 1]

    def gcol_refs(k, side):
        return g_send.at[k, slot[side]], g_in.at[k, slot[back[side]]]

    def grow_refs(k, side):
        return m_send.at[k, slot[side]], m_in.at[k, slot[back[side]]]

    kinds = {"row": (0, row_refs, ("up", "down")), "own": (1, own_refs, ("left", "right")),
             "halo": (2, halo_refs, ("left", "right")), "gcol": (3, gcol_refs, ("left", "right")),
             "grow": (4, grow_refs, ("up", "down"))}

    def copy_to(kind, k, side):
        number, refs, _ = kinds[kind]
        src, dst = refs(k, side)
        return pltpu.make_async_remote_copy(
            src_ref=src, dst_ref=dst,
            send_sem=hs_sem.at[number, k, slot[side]],
            recv_sem=hr_sem.at[number, k, slot[back[side]]],
            device_id=where_to[side], device_id_type=MESH)

    def send(kind, k):
        for side in kinds[kind][2]:
            @pl.when(have[side])
            def _():
                copy_to(kind, k, side).start()

    def receive(kind, k):
        for side in kinds[kind][2]:
            @pl.when(have[side])
            def _():
                number, refs, _ = kinds[kind]
                src, dst = refs(k, back[side])
                pltpu.make_async_remote_copy(
                    src_ref=src, dst_ref=dst,
                    send_sem=hs_sem.at[number, k, slot[back[side]]],
                    recv_sem=hr_sem.at[number, k, slot[side]],
                    device_id=where_to[side], device_id_type=MESH).wait_recv()

    def sent(kind, k):
        for side in kinds[kind][2]:
            @pl.when(have[side])
            def _():
                copy_to(kind, k, side).wait_send()

    lane = lax.broadcasted_iota(jnp.int32, (N, N), 1)
    low = lane < H
    low_h = lane[:H] < H

    def turn(x):
        return pltpu.roll(x, H, 1)

    for k in range(K):
        send("row", k)
    for k in range(K):
        re, im = obj[k, 0], obj[k, 1]
        col_send[k, 0, 0] = jnp.where(low, re, turn(im))
        col_send[k, 1, 0] = jnp.where(low, turn(re), im)
        send("own", k)

    for side, buffers in (("up", (row_in, m_in)), ("down", (row_in, m_in)),
                          ("left", (col_in, g_in)), ("right", (col_in, g_in))):
        @pl.when(jnp.logical_not(have[side]))
        def _():
            for buffer in buffers:
                for k in range(K):
                    buffer[k, slot[side]] = jnp.zeros(buffer.shape[2:], jnp.float32)
    for s in range(S):
        for p in range(2):
            zpad[s, p, :, pl.ds(0, N), :] = jnp.zeros((2, N, N), jnp.float32)
            zpad[s, p, :, pl.ds(2 * N, N), :] = jnp.zeros((2, N, N), jnp.float32)

    ys = [jnp.clip(pos[0, 0, s, 0] - r * N, 0, N - 1) for s in range(S)]
    xs = [jnp.clip(pos[0, 0, s, 1] - c * N, 0, N - 1) for s in range(S)]
    live = [(s < cnt[0, 0]).astype(jnp.float32) for s in range(S)]

    def forward_halo(k):
        receive("row", k)
        for d in range(2):
            re, im = row_in[k, d, 0], row_in[k, d, 1]
            rows = pl.ds(d * H, H)
            col_send[k, 0, 1, rows, :] = jnp.where(low_h, re, turn(im))
            col_send[k, 1, 1, rows, :] = jnp.where(low_h, turn(re), im)
        send("halo", k)

    def assemble(k):
        receive("own", k)
        receive("halo", k)
        for start, size, mid, part, begin in (
                (0, H, lambda p: row_in[k, 0, p], 1, 0),
                (H, N, lambda p: obj[k, p], 0, 0),
                (H + N, H, lambda p: row_in[k, 1, p], 1, H)):
            left = col_in[k, 0, part, pl.ds(begin, size), :]
            right = col_in[k, 1, part, pl.ds(begin, size), :]
            mask = low if size == N else low_h
            re, im = mid(0), mid(1)
            rows = pl.ds(start, size)
            padded[k, 0, 0, rows, :] = jnp.where(mask, left, turn(re))
            padded[k, 0, 1, rows, :] = turn(jnp.where(mask, right, re))
            padded[k, 1, 0, rows, :] = turn(jnp.where(mask, im, left))
            padded[k, 1, 1, rows, :] = jnp.where(mask, turn(im), right)

    def window(k, s, p):
        rows = pl.ds(ys[s], N)
        shift = lax.rem(N - xs[s], N)
        first = pltpu.roll(padded[k, p, 0, rows, :], shift, 1)
        second = pltpu.roll(padded[k, p, 1, rows, :], shift, 1)
        return jnp.where(lane < N - xs[s], first, second)

    def sandwich(res, ims, right, left):
        x = jnp.concatenate([jnp.concatenate([a, b], axis=1) for a, b in zip(res, ims)], axis=0)
        xh, xl = split(x)
        mh, ml = mats[right, 0], mats[right, 1]
        y = dot(xh, mh) + (dot(xl, mh) + dot(xh, ml))
        y = jnp.concatenate(
            [jnp.concatenate([y[s * N:(s + 1) * N, :N] for s in range(S)], axis=1),
             jnp.concatenate([y[s * N:(s + 1) * N, N:] for s in range(S)], axis=1)], axis=0)
        yh, yl = split(y)
        mh, ml = mats[left, 0], mats[left, 1]
        z = dot(mh, yh) + (dot(mh, yl) + dot(ml, yh))
        return ([z[:N, s * N:(s + 1) * N] for s in range(S)],
                [z[N:, s * N:(s + 1) * N] for s in range(S)])

    forward_halo(0)
    for k in range(K):
        assemble(k)
        if k + 1 < K:
            forward_halo(k + 1)
        exit_re, exit_im = [], []
        for s in range(S):
            tr, ti = window(k, s, 0), window(k, s, 1)
            patch[k, s, 0] = tr
            patch[k, s, 1] = ti
            if k == 0:
                wr, wi = probe[0], probe[1]
            else:
                wr, wi = wave[k - 1, s, 0], wave[k - 1, s, 1]
            exit_re.append(wr * tr - wi * ti)
            exit_im.append(wr * ti + wi * tr)
        if k + 1 < K:
            next_re, next_im = sandwich(exit_re, exit_im, 0, 1)
            for s in range(S):
                wave[k, s, 0] = next_re[s]
                wave[k, s, 1] = next_im[s]
        else:
            far_re, far_im = sandwich(exit_re, exit_im, 2, 3)

    grad_re, grad_im = [], []
    for s in range(S):
        amplitude = jnp.sqrt(far_re[s] * far_re[s] + far_im[s] * far_im[s] + 1.0)
        factor = (2.0 * live[s]) * (amplitude - meas[0, 0, s]) / amplitude
        grad_re.append(factor * far_re[s])
        grad_im.append(factor * far_im[s])

    def fold_columns(k):
        receive("gcol", k)
        left, right = g_in[k, 0], g_in[k, 1]
        mask = jnp.concatenate([low, low], axis=0)
        add_re = jnp.where(mask, left, turn(right))
        add_im = jnp.where(mask, turn(left), right)
        for p, add in ((0, add_re), (1, add_im)):
            total = padded[k, p, 0] + add
            m_send[k, 0, p] = total[:H]
            m_send[k, 1, p] = total[H + N:]
            out[k, p] = total[H:H + N]
        send("grow", k)

    for k in range(K - 1, -1, -1):
        right, left = (3, 2) if k == K - 1 else (1, 0)
        ge_re, ge_im = sandwich(grad_re, grad_im, right, left)
        for s in range(S):
            if k == 0:
                wr, wi = probe[0], probe[1]
            else:
                wr, wi = wave[k - 1, s, 0], wave[k - 1, s, 1]
            parts = (wr * ge_re[s] + wi * ge_im[s], wr * ge_im[s] - wi * ge_re[s])
            for p in range(2):
                moved = pltpu.roll(parts[p], xs[s], 1)
                zpad[s, p, 0, pl.ds(N, N), :] = jnp.where(lane >= xs[s], moved, 0.0)
                zpad[s, p, 1, pl.ds(N, N), :] = jnp.where(lane < xs[s], moved, 0.0)
        halves = []
        for p in range(2):
            halves.append([sum(zpad[s, p, h, pl.ds(N - ys[s], 2 * N), :] for s in range(S))
                           for h in range(2)])
        (re_lo, re_hi), (im_lo, im_hi) = halves
        mask = jnp.concatenate([low, low], axis=0)
        g_send[k, 0] = jnp.where(mask, re_lo, turn(im_lo))
        g_send[k, 1] = jnp.where(mask, turn(re_hi), im_hi)
        send("gcol", k)
        padded[k, 0, 0] = turn(jnp.where(mask, re_hi, re_lo))
        padded[k, 1, 0] = turn(jnp.where(mask, im_hi, im_lo))
        new_re, new_im = [], []
        for s in range(S):
            tr, ti = patch[k, s, 0], patch[k, s, 1]
            new_re.append(tr * ge_re[s] + ti * ge_im[s])
            new_im.append(tr * ge_im[s] - ti * ge_re[s])
        grad_re, grad_im = new_re, new_im
        if k + 1 < K:
            fold_columns(k + 1)

    pg[pl.ds(0, N), :] = sum(grad_re)
    pg[pl.ds(N, N), :] = sum(grad_im)
    h1 = 2 * N // C
    owners = min(R, h1 // 8)
    h2 = h1 // owners

    def piece(index, size):
        return pl.ds(pl.multiple_of(index * size, 8), size)

    def exchange(me, peer, src, dst, send_sem, recv_sem, device):
        return pltpu.make_async_remote_copy(
            src_ref=src, dst_ref=dst, send_sem=send_sem.at[peer], recv_sem=recv_sem.at[me],
            device_id=device, device_id_type=MESH)

    def col_scatter(me, peer):
        return exchange(me, peer, pg.at[piece(peer, h1)], s1.at[me], as_sem.at[0], ar_sem.at[0], (r, peer))

    def row_scatter(me, peer):
        return exchange(me, peer, q1.at[piece(peer, h2)], s2.at[me], bs_sem.at[0], br_sem.at[0], (peer, c))

    def row_gather(me, peer):
        return exchange(me, peer, q2, f2.at[piece(me, h2)], bs_sem.at[1], br_sem.at[1], (peer, c))

    def col_gather(me, peer):
        return exchange(me, peer, f2, pg_out.at[piece(me, h1)], as_sem.at[1], ar_sem.at[1], (r, peer))

    def when_owner(index, action):
        if owners == R:
            action()
        else:
            pl.when(index < owners)(action)

    col_peers = [lax.rem(c + j, C) for j in range(1, C)]
    row_peers = [lax.rem(r + j, R) for j in range(1, R)]

    for peer in col_peers:
        col_scatter(c, peer).start()
    fold_columns(0)
    s1[c] = pg[piece(c, h1), :]
    for peer in col_peers:
        col_scatter(peer, c).wait_recv()
    q1[...] = sum(s1[j] for j in range(C))
    for peer in row_peers:
        when_owner(peer, lambda: row_scatter(r, peer).start())

    def reduce_rows():
        s2[r] = q1[piece(r, h2), :]
        for peer in row_peers:
            row_scatter(peer, r).wait_recv()
        total = sum(s2[j] for j in range(R))
        q2[...] = total
        f2[piece(r, h2), :] = total
        for peer in row_peers:
            row_gather(r, peer).start()

    when_owner(r, reduce_rows)
    for peer in row_peers:
        when_owner(peer, lambda: row_gather(peer, r).wait_recv())
    for peer in col_peers:
        col_gather(c, peer).start()
    pg_out[piece(c, h1), :] = f2[...]

    for k in range(K - 1, -1, -1):
        receive("grow", k)
        for p in range(2):
            out[k, p, pl.ds(0, H), :] += m_in[k, 0, p]
            out[k, p, pl.ds(H, H), :] += m_in[k, 1, p]

    for peer in col_peers:
        col_gather(peer, c).wait_recv()
    for kind in kinds:
        for k in range(K):
            sent(kind, k)
    for peer in col_peers:
        col_scatter(c, peer).wait_send()
        col_gather(c, peer).wait_send()
    for peer in row_peers:
        when_owner(peer, lambda: row_scatter(r, peer).wait_send())
    for peer in row_peers:
        when_owner(r, lambda: row_gather(r, peer).wait_send())


def per_device(R, C, object_field, probe_wave, positions, counts, measured):
    K, _, N, _ = object_field.shape
    S = measured.shape[2]
    H = N // 2
    f32 = jnp.float32
    h1 = 2 * N // C
    owners = min(R, h1 // 8)
    h2 = h1 // owners
    vmem = pl.BlockSpec(memory_space=pltpu.VMEM)
    smem = pl.BlockSpec(memory_space=pltpu.SMEM)
    dma = pltpu.SemaphoreType.DMA
    grad, probe_grad = pl.pallas_call(
        functools.partial(kernel, R, C),
        out_shape=(jax.ShapeDtypeStruct(object_field.shape, f32), jax.ShapeDtypeStruct((2 * N, N), f32)),
        in_specs=[smem, smem, vmem, vmem, vmem, vmem],
        out_specs=(vmem, vmem),
        scratch_shapes=[
            pltpu.VMEM((K, 2, 2, H, N), f32),
            pltpu.VMEM((K, 2, 2, N, N), f32),
            pltpu.VMEM((K, 2, 2, N, N), f32),
            pltpu.VMEM((K, 2, 2, 2 * N, N), f32),
            pltpu.VMEM((K, S, 2, N, N), f32),
            pltpu.VMEM((K - 1, S, 2, N, N), f32),
            pltpu.VMEM((S, 2, 2, 3 * N, N), f32),
            pltpu.VMEM((K, 2, 2 * N, N), f32),
            pltpu.VMEM((K, 2, 2 * N, N), f32),
            pltpu.VMEM((K, 2, 2, H, N), f32),
            pltpu.VMEM((K, 2, 2, H, N), f32),
            pltpu.VMEM((2 * N, N), f32),
            pltpu.VMEM((C, h1, N), f32),
            pltpu.VMEM((h1, N), f32),
            pltpu.VMEM((R, h2, N), f32),
            pltpu.VMEM((h2, N), f32),
            pltpu.VMEM((h1, N), f32),
            dma((5, K, 2)), dma((5, K, 2)),
            dma((2, C)), dma((2, C)),
            dma((2, R)), dma((2, R)),
        ],
        compiler_params=pltpu.CompilerParams(
            collective_id=0, has_side_effects=True, vmem_limit_bytes=40 * 1024 * 1024),
    )(positions, counts, object_field, probe_wave, measured, jnp.asarray(tables(N)))
    return grad, probe_grad.reshape(2, N, N)


def solution(mesh):
    in_specs = (
        P(None, None, "row", "col"),
        P(),
        P("row", "col", None, None),
        P("row", "col"),
        P("row", "col", None, None, None),
    )
    out_specs = (P(None, None, "row", "col"), P())
    body = functools.partial(per_device, mesh.shape["row"], mesh.shape["col"])
    return jax.shard_map(body, mesh=mesh, in_specs=in_specs, out_specs=out_specs, check_vma=False)
```

time: 376 us -> 60.4 us (0.16)
  waiting for transfers between devices: 162 us -> 0 us
  matrix products: 128 us -> 0 us
  Pallas kernels: 0 us -> 53.3 us
  local copies, waits for them, and re-layouts: 29.7 us -> 5.53 us
  starting transfers between devices: 22.4 us -> 0 us
  between operations: 14.6 us -> 1.32 us
  loops' own time: 13 us -> 0 us
    dot_general x224 -> x0, matrix products: 128 us -> none  [matmul_exact(): jnp.dot(left, right, precision=lax.Precision.HIGHEST, preferred_element_t...]
    psum x1 -> x0, waiting for transfers between devices: 117 us -> none  [per_device(): probe_grad_all = lax.psum(probe_sum, ('row', 'col'))]
    pallas_call x0 -> x1, Pallas kernels: none -> 53.3 us  [per_device(): pl.pallas_call(functools.partial(kernel, R, C), out_shape=(jax.ShapeDtype...]
    ppermute x8 -> x0, waiting for transfers between devices: 44.4 us -> none  [the longest x4 38.9 us: with_halo(): before = lax.ppermute(last, axis, up)]
    ppermute x8 -> x0, starting transfers between devices: 22.4 us -> none  [the longest x4 17.2 us: with_halo(): before = lax.ppermute(last, axis, up)]
    dynamic_update_slice x2 -> x0, local copies, waits for them, and re-layouts: 13.9 us -> none  [visit(): lax.dynamic_update_slice(object_sum, current + weight * patch_grad, starts)]
    another operation x1 -> x0, loops' own time: 13 us -> none  [per_device(): lax.fori_loop(0, local_starts.shape[0], visit, initial)]
    slice x10 -> x0, local copies, waits for them, and re-layouts: 6.86 us -> none  [the longest x2 3.07 us: position_loss(): trans_real = patch_stack[depth_index, 0]]
  transfers between devices with their start and end apart: 9 -> 0, of which waited for: 6 -> 0; matrix products, arithmetic and copies ran while one was open for 1% -> 0% of each run, Pallas kernels for 0% -> 0%
where the time goes in v1:
time: 60.4 us; the launch traced here: 60.1 us
  Pallas kernels  53.3 us (88%)
  local copies, waits for them, and re-layouts  5.53 us (9%)
  between operations  1.32 us (2%)
    pallas_call x1, Pallas kernels, per_device(): pl.pallas_call(functools.partial(kernel, R, C), out_shape=(jax.ShapeDtype...  53.3 us
    unnamed x12, local copies, waits for them, and re-layouts  5.53 us

profile of v1, /device:TPU:0, one launch (start us, length us, event | category | flops | bytes accessed | tf_op | source)
XLA Modules:
  0.0 60.1 jit_solution(3328727786319284938)
XLA Ops:
  0.6 0.0 copy-start.4
  1.3 0.0 copy-done.4
  1.3 0.0 copy-start
  1.3 1.2 %copy-done = bf16[4,2,256,256]{3,2,1,0:T(8,128)(2,1)S(1)} copy-done((bf16[4,2,256,256]{3,2,1,0:T(8,128)(2,1)S(1)}, bf16[4,2,256,256]{3,2,1,0:T(8,128)(2,1)}, u32[]{:S(2)}) %copy-start) | copy-done | bytes 1048600
  2.5 0.0 copy-start.1
  2.5 1.0 %copy-done.1 = f32[4,2,128,128]{3,2,1,0:T(8,128)S(1)} copy-done((f32[4,2,128,128]{3,2,1,0:T(8,128)S(1)}, f32[4,2,128,128]{3,2,1,0:T(8,128)}, u32[]{:S(2)}) %copy-start.1) | copy-done | bytes 524312
  3.6 0.0 copy-start.2
  3.6 0.9 %copy-done.2 = f32[2,128,128]{2,1,0:T(8,128)S(1)} copy-done((f32[2,128,128]{2,1,0:T(8,128)S(1)}, f32[2,128,128]{2,1,0:T(8,128)}, u32[]{:S(2)}) %copy-start.2) | copy-done | bytes 131096
  4.5 0.0 copy-start.3
  4.5 0.9 %copy-done.3 = f32[1,1,2,128,128]{4,3,2,1,0:T(8,128)S(1)} copy-done((f32[1,1,2,128,128]{4,3,2,1,0:T(8,128)S(1)}, f32[1,1,2,128,128]{4,3,2,1,0:T(8,128)}, u32[]{:S(2)}) %copy-start.3) | copy-done | bytes 131096
  5.4 53.3 %shard_map.77 = (f32[4,2,128,128]{3,2,1,0:T(8,128)S(1)}, f32[256,128]{1,0:T(8,128)S(1)}) custom-call(s32[1,1,2,2]{3,2,1,0:T(2,128)S(1)} %copy-done.4, s32[1,1]{1,0:T(1,128)S(6)} %copy.10.cnt, f32[4,2,128,128]{3,2,1,0:T(8,128)S(1)} %copy-done.1, f32[2,128,128]{2,1,0:T(8,128)S(1)} %copy-done.2, f32[1,1,2,128,128]{4,3,2,1,0:T(8,128)S(1)} %copy-done.3, ...), custom_call_target="tpu_custom_call" | custom-call | tf_op jit(solution)/shard_map/pallas_call | solution.py:365
  58.7 0.8 %copy.11 = f32[4,2,128,128]{3,2,1,0:T(8,128)} copy(f32[4,2,128,128]{3,2,1,0:T(8,128)S(1)} %get-tuple-element.8) | data formatting | bytes 1048576
  59.5 0.7 %copy.12 = f32[2,128,128]{2,1,0:T(8,128)} copy(f32[2,128,128]{2,1,0:T(8,128)S(1)} %bitcast.1) | data formatting | bytes 262144
Async XLA Ops:
  0.6 0.7 %copy-start.4 = (s32[1,1,2,2]{3,2,1,0:T(2,128)S(1)}, s32[1,1,2,2]{3,2,1,0:T(2,128)}, u32[]{:S(2)}) copy-start(s32[1,1,2,2]{3,2,1,0:T(2,128)} %pos.1) | copy-start | bytes 52
  1.3 1.2 %copy-start = (bf16[4,2,256,256]{3,2,1,0:T(8,128)(2,1)S(1)}, bf16[4,2,256,256]{3,2,1,0:T(8,128)(2,1)}, u32[]{:S(2)}) copy-start(bf16[4,2,256,256]{3,2,1,0:T(8,128)(2,1)} %constant.2.clone.mats) | copy-start | bytes 3145732
  2.5 1.0 %copy-start.1 = (f32[4,2,128,128]{3,2,1,0:T(8,128)S(1)}, f32[4,2,128,128]{3,2,1,0:T(8,128)}, u32[]{:S(2)}) copy-start(f32[4,2,128,128]{3,2,1,0:T(8,128)} %obj.1) | copy-start | bytes 1572868
  3.6 0.9 %copy-start.2 = (f32[2,128,128]{2,1,0:T(8,128)S(1)}, f32[2,128,128]{2,1,0:T(8,128)}, u32[]{:S(2)}) copy-start(f32[2,128,128]{2,1,0:T(8,128)} %probe.1) | copy-start | bytes 393220
  4.5 0.9 %copy-start.3 = (f32[1,1,2,128,128]{4,3,2,1,0:T(8,128)S(1)}, f32[1,1,2,128,128]{4,3,2,1,0:T(8,128)}, u32[]{:S(2)}) copy-start(f32[1,1,2,128,128]{4,3,2,1,0:T(8,128)} %meas.1) | copy-start | bytes 393220

commit v2 on v1

--- a/solution.py
+++ b/solution.py
@@ -38,12 +38,13 @@
     return jnp.dot(a, b, preferred_element_type=jnp.float32)
 
 
-def kernel(R, C, pos, cnt, obj, probe, meas, mats, out, pg_out,
+def kernel(R, C, pos, cnt, obj_h, probe_h, meas_h, mats_h, out, pg_out,
+           obj, probe, meas, mats,
            row_in, col_send, col_in, padded, patch, wave, zpad, g_send, g_in, m_send, m_in,
            pg, s1, q1, s2, q2, f2,
-           hs_sem, hr_sem, as_sem, ar_sem, bs_sem, br_sem):
-    K = obj.shape[0]
-    N = obj.shape[-1]
+           hs_sem, hr_sem, as_sem, ar_sem, bs_sem, br_sem, local_sem):
+    K = obj_h.shape[0]
+    N = obj_h.shape[-1]
     H = N // 2
     S = meas.shape[2]
     r = lax.axis_index("row")
@@ -54,7 +55,13 @@
         pl.semaphore_signal(barrier, inc=1, device_id=(lax.rem(r + j, R), c), device_id_type=MESH)
     for j in range(1, C):
         pl.semaphore_signal(barrier, inc=1, device_id=(r, lax.rem(c + j, C)), device_id_type=MESH)
-    pl.semaphore_wait(barrier, R + C - 2)
+
+    fetch_obj = [pltpu.make_async_copy(obj_h.at[k], obj.at[k], local_sem.at[k]) for k in range(K)]
+    fetch_probe = pltpu.make_async_copy(probe_h, probe, local_sem.at[K])
+    fetch_meas = pltpu.make_async_copy(meas_h, meas, local_sem.at[K + 1])
+    fetch_mats = [pltpu.make_async_copy(mats_h.at[i], mats.at[i], local_sem.at[K + 2 + i]) for i in range(4)]
+    for fetch in fetch_obj + [fetch_probe] + fetch_mats + [fetch_meas]:
+        fetch.start()
 
     have = {"up": r > 0, "down": r < R - 1, "left": c > 0, "right": c < C - 1}
     where_to = {"up": (r - 1, c), "down": (r + 1, c), "left": (r, c - 1), "right": (r, c + 1)}
@@ -63,7 +70,7 @@
 
     def row_refs(k, side):
         rows = pl.ds(0, H) if side == "up" else pl.ds(H, H)
-        return obj.at[k, :, rows, :], row_in.at[k, slot[back[side]]]
+        return obj_h.at[k, :, rows, :], row_in.at[k, slot[back[side]]]
 
     def own_refs(k, side):
         return col_send.at[k, slot[side], 0], col_in.at[k, slot[back[side]], 0]
@@ -108,11 +115,14 @@
                     recv_sem=hr_sem.at[number, k, slot[side]],
                     device_id=where_to[side], device_id_type=MESH).wait_recv()
 
-    def sent(kind, k):
-        for side in kinds[kind][2]:
+    def sent():
+        for side in have:
             @pl.when(have[side])
             def _():
-                copy_to(kind, k, side).wait_send()
+                for kind in kinds:
+                    if side in kinds[kind][2]:
+                        for k in range(K):
+                            copy_to(kind, k, side).wait_send()
 
     lane = lax.broadcasted_iota(jnp.int32, (N, N), 1)
     low = lane < H
@@ -120,14 +130,6 @@
 
     def turn(x):
         return pltpu.roll(x, H, 1)
-
-    for k in range(K):
-        send("row", k)
-    for k in range(K):
-        re, im = obj[k, 0], obj[k, 1]
-        col_send[k, 0, 0] = jnp.where(low, re, turn(im))
-        col_send[k, 1, 0] = jnp.where(low, turn(re), im)
-        send("own", k)
 
     for side, buffers in (("up", (row_in, m_in)), ("down", (row_in, m_in)),
                           ("left", (col_in, g_in)), ("right", (col_in, g_in))):
@@ -141,6 +143,20 @@
             zpad[s, p, :, pl.ds(0, N), :] = jnp.zeros((2, N, N), jnp.float32)
             zpad[s, p, :, pl.ds(2 * N, N), :] = jnp.zeros((2, N, N), jnp.float32)
 
+    pl.semaphore_wait(barrier, R + C - 2)
+
+    def pack_own(k):
+        fetch_obj[k].wait()
+        re, im = obj[k, 0], obj[k, 1]
+        col_send[k, 0, 0] = jnp.where(low, re, turn(im))
+        col_send[k, 1, 0] = jnp.where(low, turn(re), im)
+        send("own", k)
+
+    send("row", 0)
+    pack_own(0)
+    send("row", 1)
+    pack_own(1)
+
     ys = [jnp.clip(pos[0, 0, s, 0] - r * N, 0, N - 1) for s in range(S)]
     xs = [jnp.clip(pos[0, 0, s, 1] - c * N, 0, N - 1) for s in range(S)]
     live = [(s < cnt[0, 0]).astype(jnp.float32) for s in range(S)]
@@ -153,6 +169,9 @@
             col_send[k, 0, 1, rows, :] = jnp.where(low_h, re, turn(im))
             col_send[k, 1, 1, rows, :] = jnp.where(low_h, turn(re), im)
         send("halo", k)
+        if k + 2 < K:
+            send("row", k + 2)
+            pack_own(k + 2)
 
     def assemble(k):
         receive("own", k)
@@ -197,6 +216,10 @@
         assemble(k)
         if k + 1 < K:
             forward_halo(k + 1)
+        if k == 0:
+            fetch_probe.wait()
+            for fetch in fetch_mats:
+                fetch.wait()
         exit_re, exit_im = [], []
         for s in range(S):
             tr, ti = window(k, s, 0), window(k, s, 1)
@@ -216,6 +239,7 @@
         else:
             far_re, far_im = sandwich(exit_re, exit_im, 2, 3)
 
+    fetch_meas.wait()
     grad_re, grad_im = [], []
     for s in range(S):
         amplitude = jnp.sqrt(far_re[s] * far_re[s] + far_im[s] * far_im[s] + 1.0)
@@ -339,9 +363,7 @@
 
     for peer in col_peers:
         col_gather(peer, c).wait_recv()
-    for kind in kinds:
-        for k in range(K):
-            sent(kind, k)
+    sent()
     for peer in col_peers:
         col_scatter(c, peer).wait_send()
         col_gather(c, peer).wait_send()
@@ -360,14 +382,19 @@
     owners = min(R, h1 // 8)
     h2 = h1 // owners
     vmem = pl.BlockSpec(memory_space=pltpu.VMEM)
+    hbm = pl.BlockSpec(memory_space=pltpu.HBM)
     smem = pl.BlockSpec(memory_space=pltpu.SMEM)
     dma = pltpu.SemaphoreType.DMA
     grad, probe_grad = pl.pallas_call(
         functools.partial(kernel, R, C),
         out_shape=(jax.ShapeDtypeStruct(object_field.shape, f32), jax.ShapeDtypeStruct((2 * N, N), f32)),
-        in_specs=[smem, smem, vmem, vmem, vmem, vmem],
+        in_specs=[smem, smem, hbm, hbm, hbm, hbm],
         out_specs=(vmem, vmem),
         scratch_shapes=[
+            pltpu.VMEM(object_field.shape, f32),
+            pltpu.VMEM(probe_wave.shape, f32),
+            pltpu.VMEM(measured.shape, f32),
+            pltpu.VMEM((4, 2, 2 * N, 2 * N), jnp.bfloat16),
             pltpu.VMEM((K, 2, 2, H, N), f32),
             pltpu.VMEM((K, 2, 2, N, N), f32),
             pltpu.VMEM((K, 2, 2, N, N), f32),
@@ -388,6 +415,7 @@
             dma((5, K, 2)), dma((5, K, 2)),
             dma((2, C)), dma((2, C)),
             dma((2, R)), dma((2, R)),
+            dma((K + 6,)),
         ],
         compiler_params=pltpu.CompilerParams(
             collective_id=0, has_side_effects=True, vmem_limit_bytes=40 * 1024 * 1024),

time: 60.4 us -> 58.6 us (0.970)
  Pallas kernels: 53.3 us -> 51.5 us
    pallas_call x1, Pallas kernels: 53.3 us -> 51.5 us  [per_device(): pl.pallas_call(functools.partial(kernel, R, C), out_shape=(jax.ShapeDtype...]
where the time goes in v2:
time: 58.6 us; the launch traced here: 58.4 us
  Pallas kernels  51.5 us (88%)
  local copies, waits for them, and re-layouts  5.53 us (9%)
  between operations  1.32 us (2%)
    pallas_call x1, Pallas kernels, per_device(): pl.pallas_call(functools.partial(kernel, R, C), out_shape=(jax.ShapeDtype...  51.5 us
    unnamed x12, local copies, waits for them, and re-layouts  5.53 us

profile of v2, /device:TPU:0, one launch (start us, length us, event | category | flops | bytes accessed | tf_op | source)
XLA Modules:
  0.0 58.4 jit_solution(4744158676777888415)
XLA Ops:
  0.6 0.0 copy-start.4
  1.3 0.0 copy-done.4
  1.3 0.0 copy-start
  1.3 1.2 %copy-done = bf16[4,2,256,256]{3,2,1,0:T(8,128)(2,1)S(1)} copy-done((bf16[4,2,256,256]{3,2,1,0:T(8,128)(2,1)S(1)}, bf16[4,2,256,256]{3,2,1,0:T(8,128)(2,1)}, u32[]{:S(2)}) %copy-start) | copy-done | bytes 1048600
  2.5 0.0 copy-start.1
  2.5 1.0 %copy-done.1 = f32[4,2,128,128]{3,2,1,0:T(8,128)S(1)} copy-done((f32[4,2,128,128]{3,2,1,0:T(8,128)S(1)}, f32[4,2,128,128]{3,2,1,0:T(8,128)}, u32[]{:S(2)}) %copy-start.1) | copy-done | bytes 524312
  3.6 0.0 copy-start.2
  3.6 0.9 %copy-done.2 = f32[2,128,128]{2,1,0:T(8,128)S(1)} copy-done((f32[2,128,128]{2,1,0:T(8,128)S(1)}, f32[2,128,128]{2,1,0:T(8,128)}, u32[]{:S(2)}) %copy-start.2) | copy-done | bytes 131096
  4.5 0.0 copy-start.3
  4.5 0.9 %copy-done.3 = f32[1,1,2,128,128]{4,3,2,1,0:T(8,128)S(1)} copy-done((f32[1,1,2,128,128]{4,3,2,1,0:T(8,128)S(1)}, f32[1,1,2,128,128]{4,3,2,1,0:T(8,128)}, u32[]{:S(2)}) %copy-start.3) | copy-done | bytes 131096
  5.4 51.5 %shard_map.77 = (f32[4,2,128,128]{3,2,1,0:T(8,128)S(1)}, f32[256,128]{1,0:T(8,128)S(1)}) custom-call(s32[1,1,2,2]{3,2,1,0:T(2,128)S(1)} %copy-done.4, s32[1,1]{1,0:T(1,128)S(6)} %copy.10.cnt, f32[4,2,128,128]{3,2,1,0:T(8,128)S(1)} %copy-done.1, f32[2,128,128]{2,1,0:T(8,128)S(1)} %copy-done.2, f32[1,1,2,128,128]{4,3,2,1,0:T(8,128)S(1)} %copy-done.3, ...), custom_call_target="tpu_custom_call" | custom-call | tf_op jit(solution)/shard_map/pallas_call | solution.py:388
  56.9 0.8 %copy.11 = f32[4,2,128,128]{3,2,1,0:T(8,128)} copy(f32[4,2,128,128]{3,2,1,0:T(8,128)S(1)} %get-tuple-element.8) | data formatting | bytes 1048576
  57.7 0.7 %copy.12 = f32[2,128,128]{2,1,0:T(8,128)} copy(f32[2,128,128]{2,1,0:T(8,128)S(1)} %bitcast.1) | data formatting | bytes 262144
Async XLA Ops:
  0.6 0.7 %copy-start.4 = (s32[1,1,2,2]{3,2,1,0:T(2,128)S(1)}, s32[1,1,2,2]{3,2,1,0:T(2,128)}, u32[]{:S(2)}) copy-start(s32[1,1,2,2]{3,2,1,0:T(2,128)} %pos.1) | copy-start | bytes 52
  1.3 1.2 %copy-start = (bf16[4,2,256,256]{3,2,1,0:T(8,128)(2,1)S(1)}, bf16[4,2,256,256]{3,2,1,0:T(8,128)(2,1)}, u32[]{:S(2)}) copy-start(bf16[4,2,256,256]{3,2,1,0:T(8,128)(2,1)} %constant.2.clone.mats_h) | copy-start | bytes 3145732
  2.5 1.0 %copy-start.1 = (f32[4,2,128,128]{3,2,1,0:T(8,128)S(1)}, f32[4,2,128,128]{3,2,1,0:T(8,128)}, u32[]{:S(2)}) copy-start(f32[4,2,128,128]{3,2,1,0:T(8,128)} %obj_h.1) | copy-start | bytes 1572868
  3.6 0.9 %copy-start.2 = (f32[2,128,128]{2,1,0:T(8,128)S(1)}, f32[2,128,128]{2,1,0:T(8,128)}, u32[]{:S(2)}) copy-start(f32[2,128,128]{2,1,0:T(8,128)} %probe_h.1) | copy-start | bytes 393220
  4.5 0.9 %copy-start.3 = (f32[1,1,2,128,128]{4,3,2,1,0:T(8,128)S(1)}, f32[1,1,2,128,128]{4,3,2,1,0:T(8,128)}, u32[]{:S(2)}) copy-start(f32[1,1,2,128,128]{4,3,2,1,0:T(8,128)} %meas_h.1) | copy-start | bytes 393220

commit v3 on v2

--- a/solution.py
+++ b/solution.py
@@ -18,15 +18,7 @@
     dft = np.exp(-2j * math.pi * ((index[:, None] * index[None, :]) % points) / points) / math.sqrt(points)
     freq = np.where(index < points // 2, index, index - points).astype(np.float64)
     step = np.conj(dft) @ (np.exp(-1j * FRESNEL * freq**2)[:, None] * dft)
-    blocks = []
-    for m in (step, dft):
-        right = np.block([[m.real, m.imag], [-m.imag, m.real]])
-        left = np.block([[m.real, -m.imag], [m.imag, m.real]])
-        blocks += [right, left]
-    full = np.stack(blocks).astype(np.float32)
-    high = full.astype(jnp.bfloat16)
-    low = (full - high.astype(np.float32)).astype(jnp.bfloat16)
-    return np.stack([high, low], axis=1)
+    return np.stack([np.stack([m.real, m.imag]) for m in (step, dft)]).astype(np.float32)
 
 
 def split(x):
@@ -38,8 +30,8 @@
     return jnp.dot(a, b, preferred_element_type=jnp.float32)
 
 
-def kernel(R, C, pos, cnt, obj_h, probe_h, meas_h, mats_h, out, pg_out,
-           obj, probe, meas, mats,
+def kernel(R, C, pos, cnt, obj_h, probe_h, meas_h, tab_h, out_h, pg_h,
+           obj, probe, meas, tab, mats, out,
            row_in, col_send, col_in, padded, patch, wave, zpad, g_send, g_in, m_send, m_in,
            pg, s1, q1, s2, q2, f2,
            hs_sem, hr_sem, as_sem, ar_sem, bs_sem, br_sem, local_sem):
@@ -59,8 +51,8 @@
     fetch_obj = [pltpu.make_async_copy(obj_h.at[k], obj.at[k], local_sem.at[k]) for k in range(K)]
     fetch_probe = pltpu.make_async_copy(probe_h, probe, local_sem.at[K])
     fetch_meas = pltpu.make_async_copy(meas_h, meas, local_sem.at[K + 1])
-    fetch_mats = [pltpu.make_async_copy(mats_h.at[i], mats.at[i], local_sem.at[K + 2 + i]) for i in range(4)]
-    for fetch in fetch_obj + [fetch_probe] + fetch_mats + [fetch_meas]:
+    fetch_tab = pltpu.make_async_copy(tab_h, tab, local_sem.at[K + 2])
+    for fetch in fetch_obj + [fetch_tab, fetch_probe, fetch_meas]:
         fetch.start()
 
     have = {"up": r > 0, "down": r < R - 1, "left": c > 0, "right": c < C - 1}
@@ -143,6 +135,14 @@
             zpad[s, p, :, pl.ds(0, N), :] = jnp.zeros((2, N, N), jnp.float32)
             zpad[s, p, :, pl.ds(2 * N, N), :] = jnp.zeros((2, N, N), jnp.float32)
 
+    fetch_tab.wait()
+    for i in range(2):
+        for part, (re, im) in enumerate(zip(split(tab[i, 0]), split(tab[i, 1]))):
+            for form, (upper, lower) in enumerate(((im, -im), (-im, im))):
+                mats[2 * i + form, part, pl.ds(0, N), pl.ds(0, N)] = re
+                mats[2 * i + form, part, pl.ds(0, N), pl.ds(N, N)] = upper
+                mats[2 * i + form, part, pl.ds(N, N), pl.ds(0, N)] = lower
+                mats[2 * i + form, part, pl.ds(N, N), pl.ds(N, N)] = re
     pl.semaphore_wait(barrier, R + C - 2)
 
     def pack_own(k):
@@ -201,13 +201,13 @@
         x = jnp.concatenate([jnp.concatenate([a, b], axis=1) for a, b in zip(res, ims)], axis=0)
         xh, xl = split(x)
         mh, ml = mats[right, 0], mats[right, 1]
-        y = dot(xh, mh) + (dot(xl, mh) + dot(xh, ml))
+        y = dot(jnp.concatenate([xh, xl, xh], axis=1), jnp.concatenate([mh, mh, ml], axis=0))
         y = jnp.concatenate(
             [jnp.concatenate([y[s * N:(s + 1) * N, :N] for s in range(S)], axis=1),
              jnp.concatenate([y[s * N:(s + 1) * N, N:] for s in range(S)], axis=1)], axis=0)
         yh, yl = split(y)
         mh, ml = mats[left, 0], mats[left, 1]
-        z = dot(mh, yh) + (dot(mh, yl) + dot(ml, yh))
+        z = dot(jnp.concatenate([mh, mh, ml], axis=1), jnp.concatenate([yh, yl, yh], axis=0))
         return ([z[:N, s * N:(s + 1) * N] for s in range(S)],
                 [z[N:, s * N:(s + 1) * N] for s in range(S)])
 
@@ -218,8 +218,6 @@
             forward_halo(k + 1)
         if k == 0:
             fetch_probe.wait()
-            for fetch in fetch_mats:
-                fetch.wait()
         exit_re, exit_im = [], []
         for s in range(S):
             tr, ti = window(k, s, 0), window(k, s, 1)
@@ -316,8 +314,11 @@
     def row_gather(me, peer):
         return exchange(me, peer, q2, f2.at[piece(me, h2)], bs_sem.at[1], br_sem.at[1], (peer, c))
 
+    def pg_piece(me):
+        return pg_h.at[(me * h1) // N, piece(lax.rem(me, N // h1), h1)]
+
     def col_gather(me, peer):
-        return exchange(me, peer, f2, pg_out.at[piece(me, h1)], as_sem.at[1], ar_sem.at[1], (r, peer))
+        return exchange(me, peer, f2, pg_piece(me), as_sem.at[1], ar_sem.at[1], (r, peer))
 
     def when_owner(index, action):
         if owners == R:
@@ -353,13 +354,16 @@
         when_owner(peer, lambda: row_gather(peer, r).wait_recv())
     for peer in col_peers:
         col_gather(c, peer).start()
-    pg_out[piece(c, h1), :] = f2[...]
-
+    keep = pltpu.make_async_copy(f2, pg_piece(c), local_sem.at[K + 3])
+    keep.start()
+
+    store_out = [pltpu.make_async_copy(out.at[k], out_h.at[k], local_sem.at[K + 4 + k]) for k in range(K)]
     for k in range(K - 1, -1, -1):
         receive("grow", k)
         for p in range(2):
             out[k, p, pl.ds(0, H), :] += m_in[k, 0, p]
             out[k, p, pl.ds(H, H), :] += m_in[k, 1, p]
+        store_out[k].start()
 
     for peer in col_peers:
         col_gather(peer, c).wait_recv()
@@ -371,6 +375,8 @@
         when_owner(peer, lambda: row_scatter(r, peer).wait_send())
     for peer in row_peers:
         when_owner(r, lambda: row_gather(r, peer).wait_send())
+    for store in [keep] + store_out:
+        store.wait()
 
 
 def per_device(R, C, object_field, probe_wave, positions, counts, measured):
@@ -381,20 +387,21 @@
     h1 = 2 * N // C
     owners = min(R, h1 // 8)
     h2 = h1 // owners
-    vmem = pl.BlockSpec(memory_space=pltpu.VMEM)
     hbm = pl.BlockSpec(memory_space=pltpu.HBM)
     smem = pl.BlockSpec(memory_space=pltpu.SMEM)
     dma = pltpu.SemaphoreType.DMA
     grad, probe_grad = pl.pallas_call(
         functools.partial(kernel, R, C),
-        out_shape=(jax.ShapeDtypeStruct(object_field.shape, f32), jax.ShapeDtypeStruct((2 * N, N), f32)),
+        out_shape=(jax.ShapeDtypeStruct(object_field.shape, f32), jax.ShapeDtypeStruct(probe_wave.shape, f32)),
         in_specs=[smem, smem, hbm, hbm, hbm, hbm],
-        out_specs=(vmem, vmem),
+        out_specs=(hbm, hbm),
         scratch_shapes=[
             pltpu.VMEM(object_field.shape, f32),
             pltpu.VMEM(probe_wave.shape, f32),
             pltpu.VMEM(measured.shape, f32),
+            pltpu.VMEM((2, 2, N, N), f32),
             pltpu.VMEM((4, 2, 2 * N, 2 * N), jnp.bfloat16),
+            pltpu.VMEM(object_field.shape, f32),
             pltpu.VMEM((K, 2, 2, H, N), f32),
             pltpu.VMEM((K, 2, 2, N, N), f32),
             pltpu.VMEM((K, 2, 2, N, N), f32),
@@ -415,12 +422,12 @@
             dma((5, K, 2)), dma((5, K, 2)),
             dma((2, C)), dma((2, C)),
             dma((2, R)), dma((2, R)),
-            dma((K + 6,)),
+            dma((2 * K + 4,)),
         ],
         compiler_params=pltpu.CompilerParams(
-            collective_id=0, has_side_effects=True, vmem_limit_bytes=40 * 1024 * 1024),
+            collective_id=0, has_side_effects=True, vmem_limit_bytes=63 * 1024 * 1024),
     )(positions, counts, object_field, probe_wave, measured, jnp.asarray(tables(N)))
-    return grad, probe_grad.reshape(2, N, N)
+    return grad, probe_grad
 
 
 def solution(mesh):

time: 58.6 us -> 56.1 us (0.957)
  local copies, waits for them, and re-layouts: 5.53 us -> 2.57 us
    unnamed x12 -> x4, local copies, waits for them, and re-layouts: 5.53 us -> 2.57 us
where the time goes in v3:
time: 56.1 us; the launch traced here: 55.9 us
  Pallas kernels  52 us (93%)
  local copies, waits for them, and re-layouts  2.57 us (5%)
  between operations  1.29 us (2%)
    pallas_call x1, Pallas kernels, per_device(): pl.pallas_call(functools.partial(kernel, R, C), out_shape=(jax.ShapeDtype...  52 us
    unnamed x4, local copies, waits for them, and re-layouts  2.57 us

profile of v3, /device:TPU:0, one launch (start us, length us, event | category | flops | bytes accessed | tf_op | source)
XLA Modules:
  0.0 55.9 jit_solution(16114175304531207701)
XLA Ops:
  1.3 52.0 %shard_map.77 = (f32[4,2,128,128]{3,2,1,0:T(8,128)}, f32[2,128,128]{2,1,0:T(8,128)}) custom-call(s32[1,1,2,2]{3,2,1,0:T(2,128)} %pos.1, s32[1,1]{1,0:T(1,128)S(6)} %copy.10.cnt, f32[4,2,128,128]{3,2,1,0:T(8,128)} %obj_h.1, f32[2,128,128]{2,1,0:T(8,128)} %probe_h.1, f32[1,1,2,128,128]{4,3,2,1,0:T(8,128)} %meas_h.1, f32[2,2,128,128]{3,2,1,0:T(8,128)} %constant.2.clone.tab_h), custom_call_target="tpu_custom_call" | custom-call | tf_op jit(solution)/shard_map/pallas_call | solution.py:393
  53.3 0.0 copy-start
  53.3 1.9 %copy.11 = f32[4,2,128,128]{3,2,1,0:T(8,128)} copy(f32[4,2,128,128]{3,2,1,0:T(8,128)} %get-tuple-element.4) | data formatting | bytes 1048576
  55.2 0.0 copy-done
  55.3 0.7 %copy.12 = f32[2,128,128]{2,1,0:T(8,128)} copy(f32[2,128,128]{2,1,0:T(8,128)S(1)} %copy-done) | data formatting | bytes 262144
Async XLA Ops:
  53.3 1.9 %copy-start = (f32[2,128,128]{2,1,0:T(8,128)S(1)}, f32[2,128,128]{2,1,0:T(8,128)}, u32[]{:S(2)}) copy-start(f32[2,128,128]{2,1,0:T(8,128)} %get-tuple-element.5) | copy-start | bytes 393220

commit v4 on v3

--- a/solution.py
+++ b/solution.py
@@ -123,6 +123,18 @@
     def turn(x):
         return pltpu.roll(x, H, 1)
 
+    pl.semaphore_wait(barrier, R + C - 2)
+    send("row", 0)
+
+    def pack_own(k):
+        fetch_obj[k].wait()
+        re, im = obj[k, 0], obj[k, 1]
+        col_send[k, 0, 0] = jnp.where(low, re, turn(im))
+        col_send[k, 1, 0] = jnp.where(low, turn(re), im)
+        send("own", k)
+
+    pack_own(0)
+    send("row", 1)
     for side, buffers in (("up", (row_in, m_in)), ("down", (row_in, m_in)),
                           ("left", (col_in, g_in)), ("right", (col_in, g_in))):
         @pl.when(jnp.logical_not(have[side]))
@@ -143,18 +155,6 @@
                 mats[2 * i + form, part, pl.ds(0, N), pl.ds(N, N)] = upper
                 mats[2 * i + form, part, pl.ds(N, N), pl.ds(0, N)] = lower
                 mats[2 * i + form, part, pl.ds(N, N), pl.ds(N, N)] = re
-    pl.semaphore_wait(barrier, R + C - 2)
-
-    def pack_own(k):
-        fetch_obj[k].wait()
-        re, im = obj[k, 0], obj[k, 1]
-        col_send[k, 0, 0] = jnp.where(low, re, turn(im))
-        col_send[k, 1, 0] = jnp.where(low, turn(re), im)
-        send("own", k)
-
-    send("row", 0)
-    pack_own(0)
-    send("row", 1)
     pack_own(1)
 
     ys = [jnp.clip(pos[0, 0, s, 0] - r * N, 0, N - 1) for s in range(S)]
@@ -258,9 +258,59 @@
             out[k, p] = total[H:H + N]
         send("grow", k)
 
+    h1 = 2 * N // C
+    owners = min(R, h1 // 8)
+    h2 = h1 // owners
+
+    def piece(index, size):
+        return pl.ds(pl.multiple_of(index * size, 8), size)
+
+    def exchange(me, peer, src, dst, send_sem, recv_sem, device):
+        return pltpu.make_async_remote_copy(
+            src_ref=src, dst_ref=dst, send_sem=send_sem.at[peer], recv_sem=recv_sem.at[me],
+            device_id=device, device_id_type=MESH)
+
+    def col_scatter(me, peer):
+        return exchange(me, peer, pg.at[piece(peer, h1)], s1.at[me], as_sem.at[0], ar_sem.at[0], (r, peer))
+
+    def row_scatter(me, peer):
+        return exchange(me, peer, q1.at[piece(peer, h2)], s2.at[me], bs_sem.at[0], br_sem.at[0], (peer, c))
+
+    def row_gather(me, peer):
+        return exchange(me, peer, q2, f2.at[piece(me, h2)], bs_sem.at[1], br_sem.at[1], (peer, c))
+
+    def pg_piece(me):
+        return pg_h.at[(me * h1) // N, piece(lax.rem(me, N // h1), h1)]
+
+    def col_gather(me, peer):
+        return exchange(me, peer, f2, pg_piece(me), as_sem.at[1], ar_sem.at[1], (r, peer))
+
+    def when_owner(index, action):
+        if owners == R:
+            action()
+        else:
+            pl.when(index < owners)(action)
+
+    col_peers = [lax.rem(c + j, C) for j in range(1, C)]
+    row_peers = [lax.rem(r + j, R) for j in range(1, R)]
+
+    def start_probe(re, im):
+        pg[pl.ds(0, N), :] = sum(re)
+        pg[pl.ds(N, N), :] = sum(im)
+        for peer in col_peers:
+            col_scatter(c, peer).start()
+
     for k in range(K - 1, -1, -1):
         right, left = (3, 2) if k == K - 1 else (1, 0)
         ge_re, ge_im = sandwich(grad_re, grad_im, right, left)
+        new_re, new_im = [], []
+        for s in range(S):
+            tr, ti = patch[k, s, 0], patch[k, s, 1]
+            new_re.append(tr * ge_re[s] + ti * ge_im[s])
+            new_im.append(tr * ge_im[s] - ti * ge_re[s])
+        grad_re, grad_im = new_re, new_im
+        if k == 0:
+            start_probe(grad_re, grad_im)
         for s in range(S):
             if k == 0:
                 wr, wi = probe[0], probe[1]
@@ -282,62 +332,16 @@
         send("gcol", k)
         padded[k, 0, 0] = turn(jnp.where(mask, re_hi, re_lo))
         padded[k, 1, 0] = turn(jnp.where(mask, im_hi, im_lo))
-        new_re, new_im = [], []
-        for s in range(S):
-            tr, ti = patch[k, s, 0], patch[k, s, 1]
-            new_re.append(tr * ge_re[s] + ti * ge_im[s])
-            new_im.append(tr * ge_im[s] - ti * ge_re[s])
-        grad_re, grad_im = new_re, new_im
         if k + 1 < K:
             fold_columns(k + 1)
 
-    pg[pl.ds(0, N), :] = sum(grad_re)
-    pg[pl.ds(N, N), :] = sum(grad_im)
-    h1 = 2 * N // C
-    owners = min(R, h1 // 8)
-    h2 = h1 // owners
-
-    def piece(index, size):
-        return pl.ds(pl.multiple_of(index * size, 8), size)
-
-    def exchange(me, peer, src, dst, send_sem, recv_sem, device):
-        return pltpu.make_async_remote_copy(
-            src_ref=src, dst_ref=dst, send_sem=send_sem.at[peer], recv_sem=recv_sem.at[me],
-            device_id=device, device_id_type=MESH)
-
-    def col_scatter(me, peer):
-        return exchange(me, peer, pg.at[piece(peer, h1)], s1.at[me], as_sem.at[0], ar_sem.at[0], (r, peer))
-
-    def row_scatter(me, peer):
-        return exchange(me, peer, q1.at[piece(peer, h2)], s2.at[me], bs_sem.at[0], br_sem.at[0], (peer, c))
-
-    def row_gather(me, peer):
-        return exchange(me, peer, q2, f2.at[piece(me, h2)], bs_sem.at[1], br_sem.at[1], (peer, c))
-
-    def pg_piece(me):
-        return pg_h.at[(me * h1) // N, piece(lax.rem(me, N // h1), h1)]
-
-    def col_gather(me, peer):
-        return exchange(me, peer, f2, pg_piece(me), as_sem.at[1], ar_sem.at[1], (r, peer))
-
-    def when_owner(index, action):
-        if owners == R:
-            action()
-        else:
-            pl.when(index < owners)(action)
-
-    col_peers = [lax.rem(c + j, C) for j in range(1, C)]
-    row_peers = [lax.rem(r + j, R) for j in range(1, R)]
-
-    for peer in col_peers:
-        col_scatter(c, peer).start()
-    fold_columns(0)
     s1[c] = pg[piece(c, h1), :]
     for peer in col_peers:
         col_scatter(peer, c).wait_recv()
     q1[...] = sum(s1[j] for j in range(C))
     for peer in row_peers:
         when_owner(peer, lambda: row_scatter(r, peer).start())
+    fold_columns(0)
 
     def reduce_rows():
         s2[r] = q1[piece(r, h2), :]
@@ -377,6 +381,17 @@
         when_owner(r, lambda: row_gather(r, peer).wait_send())
     for store in [keep] + store_out:
         store.wait()
+
+
+def copy_kernel(grad, probe_grad, grad_out, probe_out, sems):
+    K = grad.shape[0]
+    copies = [pltpu.make_async_copy(grad.at[k, p], grad_out.at[k, p], sems.at[2 * k + p])
+              for k in range(K) for p in range(2)]
+    copies.append(pltpu.make_async_copy(probe_grad, probe_out, sems.at[2 * K]))
+    for copy in copies:
+        copy.start()
+    for copy in copies:
+        copy.wait()
 
 
 def per_device(R, C, object_field, probe_wave, positions, counts, measured):
@@ -427,7 +442,14 @@
         compiler_params=pltpu.CompilerParams(
             collective_id=0, has_side_effects=True, vmem_limit_bytes=63 * 1024 * 1024),
     )(positions, counts, object_field, probe_wave, measured, jnp.asarray(tables(N)))
-    return grad, probe_grad
+    return pl.pallas_call(
+        copy_kernel,
+        out_shape=(jax.ShapeDtypeStruct(grad.shape, f32), jax.ShapeDtypeStruct(probe_grad.shape, f32)),
+        in_specs=[hbm, hbm],
+        out_specs=(hbm, hbm),
+        scratch_shapes=[dma((2 * K + 1,))],
+        compiler_params=pltpu.CompilerParams(vmem_limit_bytes=63 * 1024 * 1024),
+    )(grad, probe_grad)
 
 
 def solution(mesh):

time: 56.1 us -> 73.2 us (1.30)
  Pallas kernels: 52 us -> 71.7 us
  local copies, waits for them, and re-layouts: 2.57 us -> 0 us
    pallas_call x0 -> x1, Pallas kernels: none -> 21 us  [per_device(): pl.pallas_call(copy_kernel, out_shape=(jax.ShapeDtypeStruct(grad.shape, f...]
    unnamed x4 -> x0, local copies, waits for them, and re-layouts: 2.57 us -> none
    pallas_call x1, Pallas kernels: 52 us -> 50.7 us  [per_device(): pl.pallas_call(functools.partial(kernel, R, C), out_shape=(jax.ShapeDtype...]
where the time goes in v4:
time: 73.2 us; the launch traced here: 73 us
  Pallas kernels  71.7 us (98%)
  between operations  1.29 us (2%)
    pallas_call x1, Pallas kernels, per_device(): pl.pallas_call(functools.partial(kernel, R, C), out_shape=(jax.ShapeDtype...  50.7 us
    pallas_call x1, Pallas kernels, per_device(): pl.pallas_call(copy_kernel, out_shape=(jax.ShapeDtypeStruct(grad.shape, f...  21 us

profile of v4, /device:TPU:0, one launch (start us, length us, event | category | flops | bytes accessed | tf_op | source)
XLA Modules:
  0.0 73.0 jit_solution(11361082166958341397)
XLA Ops:
  1.3 50.7 %shard_map.77 = (f32[4,2,128,128]{3,2,1,0:T(8,128)}, f32[2,128,128]{2,1,0:T(8,128)}) custom-call(s32[1,1,2,2]{3,2,1,0:T(2,128)} %pos.1, s32[1,1]{1,0:T(1,128)S(6)} %copy.8.cnt, f32[4,2,128,128]{3,2,1,0:T(8,128)} %obj_h.1, f32[2,128,128]{2,1,0:T(8,128)} %probe_h.1, f32[1,1,2,128,128]{4,3,2,1,0:T(8,128)} %meas_h.1, f32[2,2,128,128]{3,2,1,0:T(8,128)} %constant.2.clone.tab_h), custom_call_target="tpu_custom_call" | custom-call | tf_op jit(solution)/shard_map/pallas_call | solution.py:408
  52.0 21.0 %shard_map.78 = (f32[4,2,128,128]{3,2,1,0:T(8,128)}, f32[2,128,128]{2,1,0:T(8,128)}) custom-call(f32[4,2,128,128]{3,2,1,0:T(8,128)} %get-tuple-element.4.grad, f32[2,128,128]{2,1,0:T(8,128)} %get-tuple-element.5.probe_grad), custom_call_target="tpu_custom_call" | custom-call | tf_op jit(solution)/shard_map/pallas_call | solution.py:445

commit v5 on v4

--- a/solution.py
+++ b/solution.py
@@ -383,15 +383,19 @@
         store.wait()
 
 
-def copy_kernel(grad, probe_grad, grad_out, probe_out, sems):
+def copy_kernel(grad, probe_grad, grad_out, probe_out, grad_held, probe_held, in_sem, out_sem):
     K = grad.shape[0]
-    copies = [pltpu.make_async_copy(grad.at[k, p], grad_out.at[k, p], sems.at[2 * k + p])
-              for k in range(K) for p in range(2)]
-    copies.append(pltpu.make_async_copy(probe_grad, probe_out, sems.at[2 * K]))
-    for copy in copies:
-        copy.start()
-    for copy in copies:
-        copy.wait()
+    pieces = [(grad.at[k], grad_held.at[k], grad_out.at[k]) for k in range(K)]
+    pieces.append((probe_grad, probe_held, probe_out))
+    loads = [pltpu.make_async_copy(src, held, in_sem.at[i]) for i, (src, held, _) in enumerate(pieces)]
+    stores = [pltpu.make_async_copy(held, dst, out_sem.at[i]) for i, (_, held, dst) in enumerate(pieces)]
+    for load in loads:
+        load.start()
+    for load, store in zip(loads, stores):
+        load.wait()
+        store.start()
+    for store in stores:
+        store.wait()
 
 
 def per_device(R, C, object_field, probe_wave, positions, counts, measured):
@@ -447,7 +451,10 @@
         out_shape=(jax.ShapeDtypeStruct(grad.shape, f32), jax.ShapeDtypeStruct(probe_grad.shape, f32)),
         in_specs=[hbm, hbm],
         out_specs=(hbm, hbm),
-        scratch_shapes=[dma((2 * K + 1,))],
+        scratch_shapes=[
+            pltpu.VMEM(grad.shape, f32), pltpu.VMEM(probe_grad.shape, f32),
+            dma((K + 1,)), dma((K + 1,)),
+        ],
         compiler_params=pltpu.CompilerParams(vmem_limit_bytes=63 * 1024 * 1024),
     )(grad, probe_grad)
 

time: 73.2 us -> 54 us (0.74)
  Pallas kernels: 71.7 us -> 52.6 us
    pallas_call x1, Pallas kernels: 21 us -> 1.91 us  [per_device(): pl.pallas_call(copy_kernel, out_shape=(jax.ShapeDtypeStruct(grad.shape, f...]
where the time goes in v5:
time: 54 us; the launch traced here: 53.9 us
  Pallas kernels  52.6 us (97%)
  between operations  1.29 us (2%)
    pallas_call x1, Pallas kernels, per_device(): pl.pallas_call(functools.partial(kernel, R, C), out_shape=(jax.ShapeDtype...  50.7 us
    pallas_call x1, Pallas kernels, per_device(): pl.pallas_call(copy_kernel, out_shape=(jax.ShapeDtypeStruct(grad.shape, f...  1.91 us

profile of v5, /device:TPU:0, one launch (start us, length us, event | category | flops | bytes accessed | tf_op | source)
XLA Modules:
  0.0 53.9 jit_solution(311187126520976948)
XLA Ops:
  1.3 50.7 %shard_map.77 = (f32[4,2,128,128]{3,2,1,0:T(8,128)}, f32[2,128,128]{2,1,0:T(8,128)}) custom-call(s32[1,1,2,2]{3,2,1,0:T(2,128)} %pos.1, s32[1,1]{1,0:T(1,128)S(6)} %copy.8.cnt, f32[4,2,128,128]{3,2,1,0:T(8,128)} %obj_h.1, f32[2,128,128]{2,1,0:T(8,128)} %probe_h.1, f32[1,1,2,128,128]{4,3,2,1,0:T(8,128)} %meas_h.1, f32[2,2,128,128]{3,2,1,0:T(8,128)} %constant.2.clone.tab_h), custom_call_target="tpu_custom_call" | custom-call | tf_op jit(solution)/shard_map/pallas_call | solution.py:412
  52.0 1.9 %shard_map.78 = (f32[4,2,128,128]{3,2,1,0:T(8,128)}, f32[2,128,128]{2,1,0:T(8,128)}) custom-call(f32[4,2,128,128]{3,2,1,0:T(8,128)} %get-tuple-element.4.grad, f32[2,128,128]{2,1,0:T(8,128)} %get-tuple-element.5.probe_grad), custom_call_target="tpu_custom_call" | custom-call | tf_op jit(solution)/shard_map/pallas_call | solution.py:449

commit v6 on v5

--- a/solution.py
+++ b/solution.py
@@ -156,6 +156,7 @@
                 mats[2 * i + form, part, pl.ds(N, N), pl.ds(0, N)] = lower
                 mats[2 * i + form, part, pl.ds(N, N), pl.ds(N, N)] = re
     pack_own(1)
+    send("row", 2)
 
     ys = [jnp.clip(pos[0, 0, s, 0] - r * N, 0, N - 1) for s in range(S)]
     xs = [jnp.clip(pos[0, 0, s, 1] - c * N, 0, N - 1) for s in range(S)]
@@ -169,8 +170,9 @@
             col_send[k, 0, 1, rows, :] = jnp.where(low_h, re, turn(im))
             col_send[k, 1, 1, rows, :] = jnp.where(low_h, turn(re), im)
         send("halo", k)
+        if k + 3 < K:
+            send("row", k + 3)
         if k + 2 < K:
-            send("row", k + 2)
             pack_own(k + 2)
 
     def assemble(k):

time: 54 us -> 55.5 us (1.028)
  Pallas kernels: 52.6 us -> 54 us
    pallas_call x1, Pallas kernels: 50.7 us -> 52.1 us  [per_device(): pl.pallas_call(functools.partial(kernel, R, C), out_shape=(jax.ShapeDtype...]
where the time goes in v6:
time: 55.5 us; the launch traced here: 55.3 us
  Pallas kernels  54 us (97%)
  between operations  1.29 us (2%)
    pallas_call x1, Pallas kernels, per_device(): pl.pallas_call(functools.partial(kernel, R, C), out_shape=(jax.ShapeDtype...  52.1 us
    pallas_call x1, Pallas kernels, per_device(): pl.pallas_call(copy_kernel, out_shape=(jax.ShapeDtypeStruct(grad.shape, f...  1.91 us

profile of v6, /device:TPU:0, one launch (start us, length us, event | category | flops | bytes accessed | tf_op | source)
XLA Modules:
  0.0 55.3 jit_solution(5995660853786401816)
XLA Ops:
  1.3 52.1 %shard_map.77 = (f32[4,2,128,128]{3,2,1,0:T(8,128)}, f32[2,128,128]{2,1,0:T(8,128)}) custom-call(s32[1,1,2,2]{3,2,1,0:T(2,128)} %pos.1, s32[1,1]{1,0:T(1,128)S(6)} %copy.8.cnt, f32[4,2,128,128]{3,2,1,0:T(8,128)} %obj_h.1, f32[2,128,128]{2,1,0:T(8,128)} %probe_h.1, f32[1,1,2,128,128]{4,3,2,1,0:T(8,128)} %meas_h.1, f32[2,2,128,128]{3,2,1,0:T(8,128)} %constant.2.clone.tab_h), custom_call_target="tpu_custom_call" | custom-call | tf_op jit(solution)/shard_map/pallas_call | solution.py:414
  53.4 1.9 %shard_map.78 = (f32[4,2,128,128]{3,2,1,0:T(8,128)}, f32[2,128,128]{2,1,0:T(8,128)}) custom-call(f32[4,2,128,128]{3,2,1,0:T(8,128)} %get-tuple-element.4.grad, f32[2,128,128]{2,1,0:T(8,128)} %get-tuple-element.5.probe_grad), custom_call_target="tpu_custom_call" | custom-call | tf_op jit(solution)/shard_map/pallas_call | solution.py:451

commit v7 on v5

--- a/solution.py
+++ b/solution.py
@@ -134,7 +134,6 @@
         send("own", k)
 
     pack_own(0)
-    send("row", 1)
     for side, buffers in (("up", (row_in, m_in)), ("down", (row_in, m_in)),
                           ("left", (col_in, g_in)), ("right", (col_in, g_in))):
         @pl.when(jnp.logical_not(have[side]))
@@ -155,6 +154,7 @@
                 mats[2 * i + form, part, pl.ds(0, N), pl.ds(N, N)] = upper
                 mats[2 * i + form, part, pl.ds(N, N), pl.ds(0, N)] = lower
                 mats[2 * i + form, part, pl.ds(N, N), pl.ds(N, N)] = re
+    send("row", 1)
     pack_own(1)
 
     ys = [jnp.clip(pos[0, 0, s, 0] - r * N, 0, N - 1) for s in range(S)]

time: 54 us -> 54 us (level)
  no operation moved by 1% of the time
where the time goes in v7:
time: 54 us; the launch traced here: 53.9 us
  Pallas kernels  52.6 us (97%)
  between operations  1.29 us (2%)
    pallas_call x1, Pallas kernels, per_device(): pl.pallas_call(functools.partial(kernel, R, C), out_shape=(jax.ShapeDtype...  50.7 us
    pallas_call x1, Pallas kernels, per_device(): pl.pallas_call(copy_kernel, out_shape=(jax.ShapeDtypeStruct(grad.shape, f...  1.91 us

profile of v7, /device:TPU:0, one launch (start us, length us, event | category | flops | bytes accessed | tf_op | source)
XLA Modules:
  0.0 53.9 jit_solution(17459745474353985990)
XLA Ops:
  1.3 50.7 %shard_map.77 = (f32[4,2,128,128]{3,2,1,0:T(8,128)}, f32[2,128,128]{2,1,0:T(8,128)}) custom-call(s32[1,1,2,2]{3,2,1,0:T(2,128)} %pos.1, s32[1,1]{1,0:T(1,128)S(6)} %copy.8.cnt, f32[4,2,128,128]{3,2,1,0:T(8,128)} %obj_h.1, f32[2,128,128]{2,1,0:T(8,128)} %probe_h.1, f32[1,1,2,128,128]{4,3,2,1,0:T(8,128)} %meas_h.1, f32[2,2,128,128]{3,2,1,0:T(8,128)} %constant.2.clone.tab_h), custom_call_target="tpu_custom_call" | custom-call | tf_op jit(solution)/shard_map/pallas_call | solution.py:412
  52.0 1.9 %shard_map.78 = (f32[4,2,128,128]{3,2,1,0:T(8,128)}, f32[2,128,128]{2,1,0:T(8,128)}) custom-call(f32[4,2,128,128]{3,2,1,0:T(8,128)} %get-tuple-element.4.grad, f32[2,128,128]{2,1,0:T(8,128)} %get-tuple-element.5.probe_grad), custom_call_target="tpu_custom_call" | custom-call | tf_op jit(solution)/shard_map/pallas_call | solution.py:449
